TPU v7x, 128 devices: a whole 4x4x4 slice. The times are simulated.
128 devices in a mesh: dp: 8 (over z_lo, y), mp: 16 (over x, z_hi, core).
Axes of the slice: x: 4, y: 4, z: 4 (z_hi: 2, z_lo: 2; z = z_hi * 2 + z_lo), core: 2. Of those that a mesh axis runs over, the one named last changes fastest.
Arguments:
- inputs: bfloat16 [3072, 6144], P(('dp', 'mp')), may hold values from -24 to 24
- out_grad: bfloat16 [3072, 6144], P(('dp', 'mp')), may hold values from -24 to 24
- hidden_pre: bfloat16 [3072, 12288], P('dp', 'mp'), may hold values from -8 to 8
- w_in: bfloat16 [6144, 12288], P(None, 'mp'), may hold values from -0.078125 to 0.078125
- w_out: bfloat16 [12288, 6144], P('mp'), may hold values from -0.0546875 to 0.0546875
Outputs:
- input_grad: bfloat16 [3072, 6144], P(('dp', 'mp'))
- in_weight_grad: float32 [6144, 12288], P('dp', 'mp')
- out_weight_grad: float32 [12288, 6144], P('mp', 'dp')
All inputs are finite; a program needn't handle non-finite values.
Results may differ from a plain program's by a relative error of at most 0.019.
Values may be sent and summed in bfloat16 or wider, within the bound.
No kernel may reach another device: no remote copies, remote signals or barrier semaphores. Data moves between devices by JAX's collectives and lax.ppermute only.
A program may use at most 192 MiB of HBM per device.

v0:
```python
import math

import jax
import jax.numpy as jnp
from jax import lax
from jax.sharding import PartitionSpec as P

root_two_pi = math.sqrt(2.0 / math.pi)
cubic_coef = 0.044715


def gelu_parts(pre):
    inner = root_two_pi * (pre + cubic_coef * pre * pre * pre)
    tanh_part = jnp.tanh(inner)
    value = 0.5 * pre * (1.0 + tanh_part)
    slope = 0.5 * (1.0 + tanh_part) + 0.5 * pre * (1.0 - tanh_part * tanh_part) * root_two_pi * (
        1.0 + 3.0 * cubic_coef * pre * pre
    )
    return (value, slope)


def contract_rows(left, right):
    return lax.dot_general(
        left, right, (((0,), (0,)), ((), ())), preferred_element_type=jnp.float32
    )


def contract_last(left, right):
    return lax.dot_general(
        left, right, (((1,), (1,)), ((), ())), preferred_element_type=jnp.float32
    )


def per_device(inputs, out_grad, hidden_pre, w_in, w_out):
    rows_own = out_grad.shape[0]
    group = rows_own * lax.axis_size("mp")
    blocks_all = lax.axis_size("dp")
    scale = 1.0 / math.sqrt(group * blocks_all)
    value, slope = gelu_parts(hidden_pre.astype(jnp.float32))
    activation = value.astype(jnp.bfloat16)
    piece = lax.all_gather(out_grad, "mp", axis=0, tiled=True)
    out_term = contract_rows(activation, piece)
    act_grad = contract_last(piece, w_out)
    out_term, act_grad = (out_term, act_grad)
    out_weight_grad = lax.psum_scatter(
        (out_term * scale).astype(jnp.bfloat16), "dp", scatter_dimension=1, tiled=True
    ).astype(jnp.float32)
    pre_grad = (act_grad * slope).astype(jnp.bfloat16)
    pre_rows = pre_grad
    in_term = contract_rows(lax.all_gather(inputs, "mp", axis=0, tiled=True), pre_rows)
    in_weight_grad = lax.psum_scatter(
        (in_term * scale).astype(jnp.bfloat16), "dp", scatter_dimension=0, tiled=True
    ).astype(jnp.float32)
    pre_rows = pre_grad
    input_grad = lax.psum_scatter(
        contract_last(pre_rows, w_in).astype(jnp.bfloat16), "mp", scatter_dimension=0, tiled=True
    )
    return (input_grad, in_weight_grad, out_weight_grad)


def solution(mesh):
    return jax.shard_map(
        per_device,
        mesh=mesh,
        in_specs=(
            P(("dp", "mp"), None),
            P(("dp", "mp"), None),
            P("dp", "mp"),
            P(None, "mp"),
            P("mp", None),
        ),
        out_specs=(P(("dp", "mp"), None), P("dp", "mp"), P("mp", "dp")),
        check_vma=False,
    )
```

profile of v0, /device:TPU:1, one launch (start us, length us, event | category | flops | bytes accessed | tf_op | source)
XLA Modules:
  0.0 429.5 jit_solution(6730927302094838739)
XLA Ops:
  7.2 0.0 all-gather.3.cloned.1.call-start
  7.2 0.7 all-gather.3.cloned.1.call-update
  7.9 0.0 all-gather.5.cloned.1.call-start
  7.9 0.7 all-gather.5.cloned.1.call-update
  8.6 0.0 reduce-scatter.8.cloned.1.call-start
  8.7 63.3 %all-gather.3.cloned.1.call-done = bf16[384,6144]{1,0:T(8,128)(2,1)} async-done(((bf16[24,6144]{1,0:T(8,128)(2,1)}), bf16[384,6144]{1,0:T(8,128)(2,1)}) %all-gather.3.cloned.1.call-update) | async-done | bytes 4718608 | tf_op jit(solution)/shard_map/all_gather | solution.py:41
  72.0 9.7 %multiply_convert_fusion = bf16[768,6144]{1,0:T(8,128)(2,1)} fusion(bf16[384,6144]{1,0:T(8,128)(2,1)} %all-gather.3.cloned.1.call-done, bf16[384,768]{1,0:T(8,128)(2,1)} %param.7), kind=kOutput, calls=%fused_computation | convolution fusion | flops 3636264960 | bytes 14745600 | tf_op jit(solution)/shard_map/dot_general | solution.py:23
  81.7 0.0 copy-start
  81.7 0.0 reduce-scatter.8.cloned.1.call-update
  81.8 0.0 reduce-scatter.6.cloned.1.call-start
  81.8 1.0 copy-done
  82.8 9.6 %fusion.3 = bf16[384,768]{1,0:T(8,128)(2,1)S(1)} fusion(bf16[384,6144]{1,0:T(8,128)(2,1)} %all-gather.3.cloned.1.call-done, bf16[768,6144]{1,0:T(8,128)(2,1)} %param.9, bf16[384,768]{1,0:T(8,128)(2,1)S(1)} %copy-done), kind=kOutput, calls=%fused_computation.14 | convolution fusion | flops 3629776896 | bytes 15335424 | tf_op jit(solution)/shard_map/dot_general | solution.py:29
  92.4 38.6 %all-gather.5.cloned.1.call-done = bf16[384,6144]{1,0:T(8,128)(2,1)} async-done(((bf16[24,6144]{1,0:T(8,128)(2,1)}), bf16[384,6144]{1,0:T(8,128)(2,1)}) %all-gather.5.cloned.1.call-update) | async-done | bytes 4718608 | tf_op jit(solution)/shard_map/all_gather | solution.py:50
  131.0 9.9 %fusion = bf16[6144,768]{0,1:T(8,128)(2,1)} fusion(bf16[384,768]{1,0:T(8,128)(2,1)S(1)} %fusion.3, bf16[384,6144]{1,0:T(8,128)(2,1)} %all-gather.5.cloned.1.call-done), kind=kOutput, calls=%fused_computation.2 | convolution fusion | flops 3633315840 | bytes 14745600 | tf_op jit(solution)/shard_map/dot_general | solution.py:23
  140.9 0.0 reduce-scatter.6.cloned.1.call-update
  140.9 0.0 reduce-scatter.4.cloned.1.call-start
  141.0 11.8 %convolution_convert_fusion = bf16[384,6144]{1,0:T(8,128)(2,1)} fusion(bf16[384,768]{1,0:T(8,128)(2,1)S(1)} %fusion.3, bf16[6144,768]{1,0:T(8,128)(2,1)} %param.8), kind=kOutput, calls=%fused_computation.3 | convolution fusion | flops 3626237952 | bytes 14745600 | tf_op jit(solution)/shard_map/dot_general | solution.py:29
  152.7 0.0 reduce-scatter.4.cloned.1.call-update
  152.7 81.6 %reduce-scatter.8.cloned.1.call-done = bf16[768,768]{1,0:T(8,128)(2,1)} async-done(((bf16[768,6144]{1,0:T(8,128)(2,1)}), bf16[768,768]{1,0:T(8,128)(2,1)}) %reduce-scatter.8.cloned.1.call-update) | async-done | bytes 1179664 | tf_op jit(solution)/shard_map/reduce_scatter | solution.py:45
  234.4 2.8 convert_element_type.35
  237.2 100.8 %reduce-scatter.6.cloned.1.call-done = bf16[768,768]{0,1:T(8,128)(2,1)} async-done(((bf16[6144,768]{0,1:T(8,128)(2,1)}), bf16[768,768]{0,1:T(8,128)(2,1)}) %reduce-scatter.6.cloned.1.call-update) | async-done | bytes 1179664 | tf_op jit(solution)/shard_map/reduce_scatter | solution.py:51
  338.1 2.7 copy.8
  340.8 82.2 %reduce-scatter.4.cloned.1.call-done = bf16[24,6144]{1,0:T(8,128)(2,1)} async-done(((bf16[384,6144]{1,0:T(8,128)(2,1)}), bf16[24,6144]{1,0:T(8,128)(2,1)}) %reduce-scatter.4.cloned.1.call-update) | async-done | bytes 294928 | tf_op jit(solution)/shard_map/reduce_scatter | solution.py:55
Async XLA Ops:
  7.2 64.8 %all-gather.3.cloned.1.call-start = ((), (), s32[]{:S(2)}) async-start(), calls=%async_computation.3 | async-start | bytes 5013504 | tf_op jit(solution)/shard_map/all_gather | solution.py:41
  7.9 123.1 %all-gather.5.cloned.1.call-start = ((), (), s32[]{:S(2)}) async-start(), calls=%async_computation.5 | async-start | bytes 5013504 | tf_op jit(solution)/shard_map/all_gather | solution.py:50
  8.6 225.7 %reduce-scatter.8.cloned.1.call-start = ((), (), s32[]{:S(2)}) async-start(), calls=%async_computation.7 | async-start | bytes 10616832 | tf_op jit(solution)/shard_map/reduce_scatter | solution.py:45
  81.7 1.1 copy-start
  81.8 256.3 %reduce-scatter.6.cloned.1.call-start = ((), (), s32[]{:S(2)}) async-start(), calls=%async_computation.6 | async-start | bytes 10616832 | tf_op jit(solution)/shard_map/reduce_scatter | solution.py:51
  140.9 282.0 %reduce-scatter.4.cloned.1.call-start = ((), (), s32[]{:S(2)}) async-start(), calls=%async_computation.4 | async-start | bytes 5013504 | tf_op jit(solution)/shard_map/reduce_scatter | solution.py:55
Sparse Core Ops, SparseCore 0:
  10.4 61.5 all-gather.2
  74.4 56.5 all-gather.4
  133.4 100.9 reduce-scatter.7
  236.6 101.3 reduce-scatter.5
  342.6 80.3 reduce-scatter.3
where the time goes:
time: 430 us; the launch traced here: 429 us
  waiting for transfers between devices  368 us (86%)
  matrix products  40.9 us (10%)
  between operations  13.8 us (3%)
    reduce_scatter x1, waiting for transfers between devices, per_device(): lax.psum_scatter((in_term * scale).astype(jnp.bfloat16), 'dp', scatter_di...  101 us
    reduce_scatter x1, waiting for transfers between devices, per_device(): lax.psum_scatter(contract_last(pre_rows, w_in).astype(jnp.bfloat16), 'mp'...  82.2 us
    reduce_scatter x1, waiting for transfers between devices, per_device(): lax.psum_scatter((out_term * scale).astype(jnp.bfloat16), 'dp', scatter_d...  81.6 us
    all_gather x1, waiting for transfers between devices, per_device(): piece = lax.all_gather(out_grad, 'mp', axis=0, tiled=True)  63.3 us
    all_gather x1, waiting for transfers between devices, per_device(): lax.all_gather(inputs, 'mp', axis=0, tiled=True)  38.6 us
    dot_general x2, matrix products, contract_last(): lax.dot_general(left, right, (((1,), (1,)), ((), ())), preferred_element_...  21.4 us
    dot_general x2, matrix products, contract_rows(): lax.dot_general(left, right, (((0,), (0,)), ((), ())), preferred_element_...  19.6 us
  transfers between devices with their start and end apart: 5, of which 5 were waited for; matrix products, arithmetic and copies ran while one was open for 11% of the time, Pallas kernels for 0%

commit v1 on v0

v1 whole, which is shorter than its diff:
```python
import math

import jax
import jax.numpy as jnp
from jax import lax
from jax.sharding import PartitionSpec as P

root_two_pi = math.sqrt(2.0 / math.pi)
cubic_coef = 0.044715
AXES = ("dp", "mp")
NX, NY = 4, 4
BF, F32 = jnp.bfloat16, jnp.float32


def gelu_parts(pre):
    inner = root_two_pi * (pre + cubic_coef * pre * pre * pre)
    tanh_part = jnp.tanh(inner)
    value = 0.5 * pre * (1.0 + tanh_part)
    slope = 0.5 * (1.0 + tanh_part) + 0.5 * pre * (1.0 - tanh_part * tanh_part) * root_two_pi * (
        1.0 + 3.0 * cubic_coef * pre * pre
    )
    return (value, slope)


def contract_rows(left, right):
    return lax.dot_general(left, right, (((0,), (0,)), ((), ())), preferred_element_type=F32)


def contract_last(left, right):
    return lax.dot_general(left, right, (((1,), (1,)), ((), ())), preferred_element_type=F32)


def number(zl, y, x, zh, c):
    return (zl * NY + y) * 16 + x * 4 + zh * 2 + c


def hop(array, dzl=0, dy=0, dx=0, dzh=0, dc=0):
    pairs = []
    for zl in range(2):
        for y in range(NY):
            for x in range(NX):
                for zh in range(2):
                    for c in range(2):
                        there = number(zl ^ dzl, (y + dy) % NY, (x + dx) % NX, zh ^ dzh, c ^ dc)
                        pairs.append((number(zl, y, x, zh, c), there))
    return lax.ppermute(array, AXES, pairs)


def over_x(first):
    right = hop(first, dx=-1)
    left = hop(first, dx=1)
    far_a = hop(right[0], dx=-1)
    far_b = hop(left[1], dx=1)
    return jnp.stack([first, right, jnp.stack([far_a, far_b]), left])


def per_device(inputs, out_grad, hidden_pre, w_in, w_out):
    own, width = out_grad.shape
    dp = lax.axis_index("dp")
    mp = lax.axis_index("mp")
    zl, y = dp // NY, dp % NY
    x, zh, c = mp // 4, (mp // 2) % 2, mp % 2
    cols = width // 8
    hid = hidden_pre.shape[1]
    scale = 1.0 / math.sqrt(own * 128)

    rows0 = jnp.stack([out_grad, hop(out_grad, dzh=1)])
    rows0 = over_x(rows0).reshape(8 * own, width)
    rows1 = hop(rows0, dc=1)

    hp = hidden_pre.reshape(NX, 2, 2, own, hid)
    hp = jnp.where(zh == 1, hp[:, ::-1], hp)
    hp = jnp.where(c == 1, hp[:, :, ::-1], hp)
    hp = lax.dynamic_slice_in_dim(jnp.concatenate([hp, hp]), x, NX, 0)
    hp = hp.transpose(2, 0, 1, 3, 4).reshape(16 * own, hid)
    value, slope = gelu_parts(hp.astype(F32))
    activation = value.astype(BF)
    act_all = lax.all_gather(activation.reshape(16, own, hid), "dp", axis=0)

    both = jnp.stack([out_grad, inputs]).reshape(2, own, 2, NY, cols)
    keep = lax.dynamic_index_in_dim(both, zl, 2, keepdims=False)
    give = lax.dynamic_index_in_dim(both, 1 - zl, 2, keepdims=False)
    both = jnp.stack([keep, hop(give, dzl=1)])
    parts = []
    for k in range(NY):
        block = lax.dynamic_index_in_dim(both, (y + k) % NY, 3, keepdims=False)
        parts.append(hop(block, dy=k) if k else block)
    parts = jnp.stack([parts[0], parts[3], parts[2], parts[1]] * 2)
    parts = lax.dynamic_slice_in_dim(parts, NY - y, NY, 0)
    parts = jnp.where(zl == 1, parts[:, ::-1], parts)
    parts = parts.transpose(2, 1, 0, 3, 4).reshape(2, 8 * own, cols)
    wide = jnp.stack([parts, hop(parts, dzh=1)])
    og0 = over_x(wide[:, 0]).reshape(64 * own, cols)
    in0 = over_x(wide[:, 1]).reshape(64 * own, cols)
    og_cols = jnp.concatenate([og0, hop(og0, dc=1)])
    in_cols = jnp.concatenate([in0, hop(in0, dc=1)])

    pre0 = (contract_last(rows0, w_out) * slope[: 8 * own]).astype(BF)
    pre1 = (contract_last(rows1, w_out) * slope[8 * own :]).astype(BF)
    pre_grad = jnp.concatenate([pre0, pre1])
    pre_all = lax.all_gather(pre_grad.reshape(16, own, hid), "dp", axis=0)

    theirs = contract_last(pre1, w_in).astype(BF)
    mine = contract_last(pre0, w_in)
    total = (mine + hop(theirs, dc=1).astype(F32)).astype(BF).reshape(NX, 2, own, width)
    near_r = hop(total[2, 0], dx=1)
    near_l = hop(total[2, 1], dx=-1)
    to_r = jnp.stack([(total[1, 0].astype(F32) + near_r.astype(F32)).astype(BF), total[1, 1]])
    to_l = jnp.stack([total[3, 0], (total[3, 1].astype(F32) + near_l.astype(F32)).astype(BF)])
    got_l = hop(to_r, dx=1)
    got_r = hop(to_l, dx=-1)
    total = total[0].astype(F32) + got_l.astype(F32) + got_r.astype(F32)
    input_grad = (total[0] + hop(total[1].astype(BF), dzh=1).astype(F32)).astype(BF)

    act_all = act_all.transpose(1, 0, 2, 3).reshape(128 * own, hid)
    out_weight_grad = contract_rows(act_all, og_cols) * scale
    pre_all = pre_all.transpose(1, 0, 2, 3).reshape(128 * own, hid)
    in_weight_grad = contract_rows(in_cols, pre_all) * scale
    return (input_grad, in_weight_grad, out_weight_grad)


def solution(mesh):
    return jax.shard_map(
        per_device,
        mesh=mesh,
        in_specs=(
            P(("dp", "mp"), None),
            P(("dp", "mp"), None),
            P("dp", "mp"),
            P(None, "mp"),
            P("mp", None),
        ),
        out_specs=(P(("dp", "mp"), None), P("dp", "mp"), P("mp", "dp")),
        check_vma=False,
    )
```

time: 430 us -> 256 us (0.60)
  waiting for transfers between devices: 368 us -> 129 us
  starting transfers between devices: 0.2 us -> 41.6 us
  other arithmetic: 2.85 us -> 16 us
  local copies, waits for them, and re-layouts: 3.72 us -> 8.72 us
  matrix products: 40.9 us -> 45.7 us
    reduce_scatter x3 -> x0, waiting for transfers between devices: 265 us -> none  [the longest x1 101 us: per_device(): lax.psum_scatter((in_term * scale).astype(jnp.bfloat16), 'dp', scatter_di...]
    ppermute x0 -> x27, waiting for transfers between devices: none -> 129 us  [hop(): return lax.ppermute(array, AXES, pairs)]
    all_gather x2, waiting for transfers between devices: 102 us -> 0.01 us  [the longest x1 0.01 us: per_device(): act_all = lax.all_gather(activation.reshape(16, own, hid), 'dp', axis=0)]
    ppermute x0 -> x27, starting transfers between devices: none -> 41.5 us  [hop(): return lax.ppermute(array, AXES, pairs)]
    another operation x0 -> x11, other arithmetic: none -> 11.7 us  [the longest x8 9.31 us: over_x(): return jnp.stack([first, right, jnp.stack([far_a, far_b]), left])]
    dot_general x2 -> x4, matrix products: 21.4 us -> 28.2 us  [contract_last(): lax.dot_general(left, right, (((1,), (1,)), ((), ())), preferred_element_...]
    squeeze x0 -> x7, local copies, waits for them, and re-layouts: none -> 5.97 us  [the longest x3 2.49 us: over_x(): far_b = hop(left[1], dx=1)]
  transfers between devices with their start and end apart: 5 -> 29, of which waited for: 5 -> 15; matrix products, arithmetic and copies ran while one was open for 11% -> 24% of each run, Pallas kernels for 0% -> 0%
where the time goes in v1:
time: 256 us; the launch traced here: 255 us
  waiting for transfers between devices  129 us (50%)
  matrix products  45.7 us (18%)
  starting transfers between devices  41.6 us (16%)
  other arithmetic  16 us (6%)
  between operations  14.6 us (6%)
  local copies, waits for them, and re-layouts  8.72 us (3%)
    ppermute x27, waiting for transfers between devices, hop(): return lax.ppermute(array, AXES, pairs)  129 us
    ppermute x27, starting transfers between devices, hop(): return lax.ppermute(array, AXES, pairs)  41.5 us
    dot_general x4, matrix products, contract_last(): lax.dot_general(left, right, (((1,), (1,)), ((), ())), preferred_element_...  28.2 us
    dot_general x2, matrix products, contract_rows(): lax.dot_general(left, right, (((0,), (0,)), ((), ())), preferred_element_...  17.5 us
    another operation x8, other arithmetic, over_x(): return jnp.stack([first, right, jnp.stack([far_a, far_b]), left])  9.31 us
  transfers between devices with their start and end apart: 29, of which 15 were waited for; matrix products, arithmetic and copies ran while one was open for 24% of the time, Pallas kernels for 0%

profile of v1, /device:TPU:1, one launch (start us, length us, event | category | flops | bytes accessed | tf_op | source)
XLA Modules:
  0.0 255.3 jit_solution(12405841971858478124)
XLA Ops:
  7.2 4.5 %collective-permute-start = (bf16[24,6144]{1,0:T(8,128)(2,1)}, bf16[24,6144]{1,0:T(8,128)(2,1)S(1)}, u32[]{:S(2)}, u32[]{:S(2)}) collective-permute-start(bf16[24,6144]{1,0:T(8,128)(2,1)} %param.6), channel_id=1, source_target_pairs={{0,2},{1,3},{2,0},{3,1},{4,6},{5,7},{6,4},{7,5},{8,10},{9,11},{10,... | collective-permute-start | bytes 884744 | tf_op jit(solution)/shard_map/ppermute | solution.py:46
  11.7 6.9 %collective-permute-done = bf16[24,6144]{1,0:T(8,128)(2,1)S(1)} collective-permute-done((bf16[24,6144]{1,0:T(8,128)(2,1)}, bf16[24,6144]{1,0:T(8,128)(2,1)S(1)}, u32[]{:S(2)}, u32[]{:S(2)}) %collective-permute-start) | collective-permute-done | bytes 294944 | tf_op jit(solution)/shard_map/ppermute | solution.py:46
  18.7 1.0 fusion.54
  19.7 1.3 collective-permute-start.3
  21.0 1.2 stack.145
  22.6 1.5 collective-permute-start.1
  24.1 10.4 %collective-permute-done.3 = bf16[2,24,6144]{2,1,0:T(8,128)(2,1)S(1)} collective-permute-done((bf16[2,24,6144]{2,1,0:T(8,128)(2,1)S(1)}, bf16[2,24,6144]{2,1,0:T(8,128)(2,1)S(1)}, u32[]{:S(2)}, u32[]{:S(2)}) %collective-permute-start.3) | collective-permute-done | bytes 589856 | tf_op jit(solution)/shard_map/ppermute | solution.py:46
  36.7 2.7 %collective-permute-start.2 = (bf16[24,6144]{1,0:T(8,128)(2,1)}, bf16[24,6144]{1,0:T(8,128)(2,1)}, u32[]{:S(2)}, u32[]{:S(2)}) collective-permute-start(bf16[24,6144]{1,0:T(8,128)(2,1)} %slice_bitcast_fusion.12), channel_id=1, source_target_pairs={{0,12},{1,13},{2,14},{3,15},{4,0},{5,1},{6,2},{7,3},{8,4},{9,5},{1... | collective-permute-start | bytes 884744 | tf_op jit(solution)/shard_map/ppermute | solution.py:46
  40.7 2.5 collective-permute-done.4
  43.6 1.1 maximum_bitcast_fusion
  44.7 1.7 pad_maximum_fusion
  46.4 3.4 %collective-permute-start.5 = (bf16[192,6144]{1,0:T(8,128)(2,1)}, bf16[192,6144]{1,0:T(8,128)(2,1)}, u32[]{:S(2)}, u32[]{:S(2)}) collective-permute-start(bf16[192,6144]{1,0:T(8,128)(2,1)} %bitcast.10), channel_id=1, source_target_pairs={{0,1},{1,0},{2,3},{3,2},{4,5},{5,4},{6,7},{7,6},{8,9},{9,8},{10,11... | collective-permute-start | bytes 7077896 | tf_op jit(solution)/shard_map/ppermute | solution.py:46
  50.1 1.2 fusion.25
  51.5 2.8 %collective-permute-start.13 = (bf16[2,2,24,768]{3,2,1,0:T(8,128)(2,1)S(1)}, bf16[2,2,24,768]{3,2,1,0:T(8,128)(2,1)S(1)}, u32[]{:S(2)}, u32[]{:S(2)}) collective-permute-start(bf16[2,2,24,768]{3,2,1,0:T(8,128)(2,1)S(1)} %get-tuple-element.14), channel_id=1, source_target_pairs={{0,48},{1,49},{2,50},{3,51},{4,52},{5,53},{6,54},{7,55},{8,56},{9,... | collective-permute-start | bytes 442376 | tf_op jit(solution)/shard_map/ppermute | solution.py:46
  56.2 4.4 %collective-permute-done.13 = bf16[2,2,24,768]{3,2,1,0:T(8,128)(2,1)S(1)} collective-permute-done((bf16[2,2,24,768]{3,2,1,0:T(8,128)(2,1)S(1)}, bf16[2,2,24,768]{3,2,1,0:T(8,128)(2,1)S(1)}, u32[]{:S(2)}, u32[]{:S(2)}) %collective-permute-start.13) | collective-permute-done | bytes 147488 | tf_op jit(solution)/shard_map/ppermute | solution.py:46
  60.6 1.2 collective-permute-done.14
  61.8 4.3 %collective-permute-done.15 = bf16[2,2,24,768]{3,2,1,0:T(8,128)(2,1)S(1)} collective-permute-done((bf16[2,2,24,768]{3,2,1,0:T(8,128)(2,1)S(1)}, bf16[2,2,24,768]{3,2,1,0:T(8,128)(2,1)S(1)}, u32[]{:S(2)}, u32[]{:S(2)}) %collective-permute-start.15) | collective-permute-done | bytes 147488 | tf_op jit(solution)/shard_map/ppermute | solution.py:46
  66.3 7.9 %fusion.15 = bf16[192,768]{1,0:T(8,128)(2,1)S(1)} fusion(bf16[192,6144]{1,0:T(8,128)(2,1)} %collective-permute-done.5, bf16[768,6144]{1,0:T(8,128)(2,1)} %param.9, f32[384,768]{1,0:T(8,128)S(1)} %fusion.20), kind=kOutput, calls=%fused_computation.21 | convolution fusion | flops 1812234240 | bytes 12681216 | tf_op jit(solution)/shard_map/dot_general | solution.py:30
  74.2 8.5 %convolution_convert_fusion = bf16[192,6144]{1,0:T(8,128)(2,1)} fusion(bf16[192,768]{1,0:T(8,128)(2,1)S(1)} %fusion.15, bf16[6144,768]{1,0:T(8,128)(2,1)} %param.8), kind=kOutput, calls=%fused_computation | convolution fusion | flops 1813118976 | bytes 12091392 | tf_op jit(solution)/shard_map/dot_general | solution.py:30
  83.6 1.9 collective-permute-start.16
  85.5 39.0 %collective-permute-done.16 = bf16[2,192,768]{2,1,0:T(8,128)(2,1)S(1)} collective-permute-done((bf16[2,192,768]{2,1,0:T(8,128)(2,1)S(1)}, bf16[2,192,768]{2,1,0:T(8,128)(2,1)S(1)}, u32[]{:S(2)}, u32[]{:S(2)}) %collective-permute-start.16) | collective-permute-done | bytes 589856 | tf_op jit(solution)/shard_map/ppermute | solution.py:46
  124.6 1.0 fusion.48
  126.4 2.6 %collective-permute-start.17 = (bf16[2,192,768]{2,1,0:T(8,128)(2,1)}, bf16[2,192,768]{2,1,0:T(8,128)(2,1)}, u32[]{:S(2)}, u32[]{:S(2)}) collective-permute-start(bf16[2,192,768]{2,1,0:T(8,128)(2,1)} %get-tuple-element.10), channel_id=1, source_target_pairs={{0,12},{1,13},{2,14},{3,15},{4,0},{5,1},{6,2},{7,3},{8,4},{9,5},{1... | collective-permute-start | bytes 1769480 | tf_op jit(solution)/shard_map/ppermute | solution.py:46
  129.0 2.7 %collective-permute-start.22 = (bf16[2,192,768]{2,1,0:T(8,128)(2,1)S(1)}, bf16[2,192,768]{2,1,0:T(8,128)(2,1)S(1)}, u32[]{:S(2)}, u32[]{:S(2)}) collective-permute-start(bf16[2,192,768]{2,1,0:T(8,128)(2,1)S(1)} %get-tuple-element.11), channel_id=1, source_target_pairs={{0,12},{1,13},{2,14},{3,15},{4,0},{5,1},{6,2},{7,3},{8,4},{9,5},{1... | collective-permute-start | bytes 1769480 | tf_op jit(solution)/shard_map/ppermute | solution.py:46
  131.7 4.9 %fusion.14 = bf16[192,768]{1,0:T(8,128)(2,1)S(1)} fusion(bf16[192,6144]{1,0:T(8,128)(2,1)} %bitcast.10, bf16[768,6144]{1,0:T(8,128)(2,1)S(1)} %bitcast.169, f32[384,768]{1,0:T(8,128)S(1)} %fusion.20), kind=kOutput, calls=%fused_computation.20 | convolution fusion | flops 1812234240 | bytes 12681216 | tf_op jit(solution)/shard_map/dot_general | solution.py:30
  136.6 18.5 %collective-permute-done.24 = bf16[2,192,768]{2,1,0:T(8,128)(2,1)S(1)} collective-permute-done((bf16[2,192,768]{2,1,0:T(8,128)(2,1)S(1)}, bf16[2,192,768]{2,1,0:T(8,128)(2,1)S(1)}, u32[]{:S(2)}, u32[]{:S(2)}) %collective-permute-start.24) | collective-permute-done | bytes 589856 | tf_op jit(solution)/shard_map/ppermute | solution.py:46
  156.1 6.9 %add_convert_fusion = bf16[192,6144]{1,0:T(8,128)(2,1)S(1)} fusion(bf16[192,6144]{1,0:T(8,128)(2,1)S(1)} %collective-permute-done.6, bf16[192,768]{1,0:T(8,128)(2,1)S(1)} %fusion.14, bf16[6144,768]{1,0:T(8,128)(2,1)} %param.8), kind=kOutput, calls=%fused_computation.9 | convolution fusion | flops 1815478272 | bytes 14450688 | tf_op jit(solution)/shard_map/dot_general | solution.py:30
  163.0 1.0 slice_bitcast_fusion.9
  164.0 2.7 %collective-permute-start.9 = (bf16[24,6144]{1,0:T(8,128)(2,1)}, bf16[24,6144]{1,0:T(8,128)(2,1)}, u32[]{:S(2)}, u32[]{:S(2)}) collective-permute-start(bf16[24,6144]{1,0:T(8,128)(2,1)} %get-tuple-element.6), channel_id=1, source_target_pairs={{0,12},{1,13},{2,14},{3,15},{4,0},{5,1},{6,2},{7,3},{8,4},{9,5},{1... | collective-permute-start | bytes 884744 | tf_op jit(solution)/shard_map/ppermute | solution.py:46
  167.4 0.9 pad_maximum_fusion.7
  168.3 4.8 %collective-permute-done.7 = bf16[24,6144]{1,0:T(8,128)(2,1)} collective-permute-done((bf16[24,6144]{1,0:T(8,128)(2,1)}, bf16[24,6144]{1,0:T(8,128)(2,1)}, u32[]{:S(2)}, u32[]{:S(2)}) %collective-permute-start.7) | collective-permute-done | bytes 294944 | tf_op jit(solution)/shard_map/ppermute | solution.py:46
  173.1 1.0 collective-permute-start.23
  174.1 1.2 fusion.37
  175.4 1.1 pad_maximum_fusion.6
  176.5 1.4 collective-permute-start.10
  178.1 1.0 slice_bitcast_fusion.3
  179.6 1.0 slice_bitcast_fusion.4
  180.6 2.3 collective-permute-start.18
  182.9 1.0 maximum_bitcast_fusion.2
  184.3 3.7 %collective-permute-start.26 = (bf16[1536,768]{1,0:T(8,128)(2,1)S(1)}, bf16[1536,768]{1,0:T(8,128)(2,1)}, u32[]{:S(2)}, u32[]{:S(2)}) collective-permute-start(bf16[1536,768]{1,0:T(8,128)(2,1)S(1)} %bitcast.153), channel_id=1, source_target_pairs={{0,1},{1,0},{2,3},{3,2},{4,5},{5,4},{6,7},{7,6},{8,9},{9,8},{10,11... | collective-permute-start | bytes 7077896 | tf_op jit(solution)/shard_map/ppermute | solution.py:46
  188.0 4.7 %collective-permute-done.10 = bf16[2,24,6144]{2,1,0:T(8,128)(2,1)S(1)} collective-permute-done((bf16[2,24,6144]{2,1,0:T(8,128)(2,1)S(1)}, bf16[2,24,6144]{2,1,0:T(8,128)(2,1)S(1)}, u32[]{:S(2)}, u32[]{:S(2)}) %collective-permute-start.10) | collective-permute-done | bytes 589856 | tf_op jit(solution)/shard_map/ppermute | solution.py:46
  193.6 4.4 %collective-permute-done.20 = bf16[192,768]{1,0:T(8,128)(2,1)S(1)} collective-permute-done((bf16[192,768]{1,0:T(8,128)(2,1)S(1)}, bf16[192,768]{1,0:T(8,128)(2,1)S(1)}, u32[]{:S(2)}, u32[]{:S(2)}) %collective-permute-start.20) | collective-permute-done | bytes 294944 | tf_op jit(solution)/shard_map/ppermute | solution.py:46
  198.0 1.0 collective-permute-done.18
  199.1 3.1 %pad_maximum_fusion.1 = bf16[4,2,192,768]{3,2,1,0:T(8,128)(2,1)} fusion(bf16[1,2,192,768]{3,2,1,0:T(8,128)(2,1)} %bitcast.49, bf16[1,2,192,768]{3,2,1,0:T(8,128)(2,1)S(1)} %maximum_bitcast_fusion.1, bf16[1,2,192,768]{3,2,1,0:T(8,128)(2,1)} %bitcast.43, bf16[1,2,192,768]{3,2,1,0:T(8,128)(2,1)S(1)} %get-tuple-element.12), kind=kLoop, calls=%fused_computation.11 | loop fusion | flops 3538944 | bytes 4718592 | tf_op jit(solution)/shard_map/stack | solution.py:54
  202.2 2.7 %collective-permute-start.21 = (bf16[1536,768]{1,0:T(8,128)(2,1)}, bf16[1536,768]{1,0:T(8,128)(2,1)}, u32[]{:S(2)}, u32[]{:S(2)}) collective-permute-start(bf16[1536,768]{1,0:T(8,128)(2,1)} %bitcast.50), channel_id=1, source_target_pairs={{0,1},{1,0},{2,3},{3,2},{4,5},{5,4},{6,7},{7,6},{8,9},{9,8},{10,11... | collective-permute-start | bytes 7077896 | tf_op jit(solution)/shard_map/ppermute | solution.py:46
  204.9 25.4 %collective-permute-done.11 = bf16[24,6144]{1,0:T(8,128)(2,1)S(1)} collective-permute-done((bf16[24,6144]{1,0:T(8,128)(2,1)S(1)}, bf16[24,6144]{1,0:T(8,128)(2,1)S(1)}, u32[]{:S(2)}, u32[]{:S(2)}) %collective-permute-start.11) | collective-permute-done | bytes 294944 | tf_op jit(solution)/shard_map/ppermute | solution.py:46
  231.0 8.4 %fusion.8 = f32[768,768]{1,0:T(8,128)} fusion(bf16[3072,768]{1,0:T(8,128)(2,1)} %bitcast.170, bf16[1536,768]{1,0:T(8,128)(2,1)} %collective-permute-done.26, bf16[1536,768]{1,0:T(8,128)(2,1)S(1)} %bitcast.154), kind=kOutput, calls=%fused_computation.13 | convolution fusion | flops 3633905664 | bytes 11796480 | tf_op jit(solution)/shard_map/dot_general | solution.py:26
  239.4 9.1 %fusion.11 = f32[768,768]{1,0:T(8,128)} fusion(bf16[3072,768]{1,0:T(8,128)(2,1)} %bitcast.171, bf16[1536,768]{1,0:T(8,128)(2,1)} %collective-permute-done.21, bf16[1536,768]{1,0:T(8,128)(2,1)} %bitcast.50), kind=kOutput, calls=%fused_computation.17 | convolution fusion | flops 3633905664 | bytes 11796480 | tf_op jit(solution)/shard_map/dot_general | solution.py:26
  (89 shorter events, 12.8 us)
Async XLA Ops:
  7.2 15.1 %copy-start.8 = (bf16[24,6144]{1,0:T(8,128)(2,1)S(1)}, bf16[24,6144]{1,0:T(8,128)(2,1)}, u32[]{:S(2)}) copy-start(bf16[24,6144]{1,0:T(8,128)(2,1)} %param.5) | copy-start | bytes 884740
  7.2 223.8 %all-gather.5.cloned.1.call-start = ((), (), s32[]{:S(2)}) async-start(), calls=%async_computation.1 | async-start | bytes 5308416 | tf_op jit(solution)/shard_map/all_gather | solution.py:78
  7.2 11.5 %collective-permute-start = (bf16[24,6144]{1,0:T(8,128)(2,1)}, bf16[24,6144]{1,0:T(8,128)(2,1)S(1)}, u32[]{:S(2)}, u32[]{:S(2)}) collective-permute-start(bf16[24,6144]{1,0:T(8,128)(2,1)} %param.6), channel_id=1, source_target_pairs={{0,2},{1,3},{2,0},{3,1},{4,6},{5,7},{6,4},{7,5},{8,10},{9,11},{10,... | collective-permute-start | bytes 884744 | tf_op jit(solution)/shard_map/ppermute | solution.py:46
  19.7 14.9 %collective-permute-start.3 = (bf16[2,24,6144]{2,1,0:T(8,128)(2,1)S(1)}, bf16[2,24,6144]{2,1,0:T(8,128)(2,1)S(1)}, u32[]{:S(2)}, u32[]{:S(2)}) collective-permute-start(bf16[2,24,6144]{2,1,0:T(8,128)(2,1)S(1)} %get-tuple-element.19), channel_id=1, source_target_pairs={{0,4},{1,5},{2,6},{3,7},{4,8},{5,9},{6,10},{7,11},{8,12},{9,13},{1... | collective-permute-start | bytes 1769480 | tf_op jit(solution)/shard_map/ppermute | solution.py:46
  21.0 19.5 %copy-start.7 = (bf16[384,768]{1,0:T(8,128)(2,1)S(1)}, bf16[384,768]{1,0:T(8,128)(2,1)}, u32[]{:S(2)}) copy-start(bf16[384,768]{1,0:T(8,128)(2,1)} %param.7) | copy-start | bytes 1769476
  22.6 13.4 %collective-permute-start.1 = (bf16[2,24,6144]{2,1,0:T(8,128)(2,1)S(1)}, bf16[2,24,6144]{2,1,0:T(8,128)(2,1)S(1)}, u32[]{:S(2)}, u32[]{:S(2)}) collective-permute-start(bf16[2,24,6144]{2,1,0:T(8,128)(2,1)S(1)} %get-tuple-element.19), channel_id=1, source_target_pairs={{0,12},{1,13},{2,14},{3,15},{4,0},{5,1},{6,2},{7,3},{8,4},{9,5},{1... | collective-permute-start | bytes 1769480 | tf_op jit(solution)/shard_map/ppermute | solution.py:46
  35.3 7.9 %collective-permute-start.4 = (bf16[24,6144]{1,0:T(8,128)(2,1)}, bf16[24,6144]{1,0:T(8,128)(2,1)}, u32[]{:S(2)}, u32[]{:S(2)}) collective-permute-start(bf16[24,6144]{1,0:T(8,128)(2,1)} %slice_bitcast_fusion.11), channel_id=1, source_target_pairs={{0,4},{1,5},{2,6},{3,7},{4,8},{5,9},{6,10},{7,11},{8,12},{9,13},{1... | collective-permute-start | bytes 884744 | tf_op jit(solution)/shard_map/ppermute | solution.py:46
  36.7 6.9 %collective-permute-start.2 = (bf16[24,6144]{1,0:T(8,128)(2,1)}, bf16[24,6144]{1,0:T(8,128)(2,1)}, u32[]{:S(2)}, u32[]{:S(2)}) collective-permute-start(bf16[24,6144]{1,0:T(8,128)(2,1)} %slice_bitcast_fusion.12), channel_id=1, source_target_pairs={{0,12},{1,13},{2,14},{3,15},{4,0},{5,1},{6,2},{7,3},{8,4},{9,5},{1... | collective-permute-start | bytes 884744 | tf_op jit(solution)/shard_map/ppermute | solution.py:46
  40.1 11.3 %collective-permute-start.12 = (bf16[2,24,4,768]{3,1,0,2:T(8,128)(2,1)}, bf16[2,24,4,768]{3,1,0,2:T(8,128)(2,1)S(1)}, u32[]{:S(2)}, u32[]{:S(2)}) collective-permute-start(bf16[2,24,4,768]{3,1,0,2:T(8,128)(2,1)} %get-tuple-element.17), channel_id=1, source_target_pairs={{0,64},{1,65},{2,66},{3,67},{4,68},{5,69},{6,70},{7,71},{8,72},{9,... | collective-permute-start | bytes 884744 | tf_op jit(solution)/shard_map/ppermute | solution.py:46
  46.4 19.8 %collective-permute-start.5 = (bf16[192,6144]{1,0:T(8,128)(2,1)}, bf16[192,6144]{1,0:T(8,128)(2,1)}, u32[]{:S(2)}, u32[]{:S(2)}) collective-permute-start(bf16[192,6144]{1,0:T(8,128)(2,1)} %bitcast.10), channel_id=1, source_target_pairs={{0,1},{1,0},{2,3},{3,2},{4,5},{5,4},{6,7},{7,6},{8,9},{9,8},{10,11... | collective-permute-start | bytes 7077896 | tf_op jit(solution)/shard_map/ppermute | solution.py:46
  51.3 188.1 %all-gather.3.cloned.1.call-start = ((), (), s32[]{:S(2)}) async-start(), calls=%async_computation | async-start | bytes 5308416 | tf_op jit(solution)/shard_map/all_gather | solution.py:101
  51.5 9.1 %collective-permute-start.13 = (bf16[2,2,24,768]{3,2,1,0:T(8,128)(2,1)S(1)}, bf16[2,2,24,768]{3,2,1,0:T(8,128)(2,1)S(1)}, u32[]{:S(2)}, u32[]{:S(2)}) collective-permute-start(bf16[2,2,24,768]{3,2,1,0:T(8,128)(2,1)S(1)} %get-tuple-element.14), channel_id=1, source_target_pairs={{0,48},{1,49},{2,50},{3,51},{4,52},{5,53},{6,54},{7,55},{8,56},{9,... | collective-permute-start | bytes 442376 | tf_op jit(solution)/shard_map/ppermute | solution.py:46
  55.0 6.8 %collective-permute-start.14 = (bf16[2,2,24,768]{3,2,1,0:T(8,128)(2,1)S(1)}, bf16[2,2,24,768]{3,2,1,0:T(8,128)(2,1)S(1)}, u32[]{:S(2)}, u32[]{:S(2)}) collective-permute-start(bf16[2,2,24,768]{3,2,1,0:T(8,128)(2,1)S(1)} %get-tuple-element.15), channel_id=1, source_target_pairs={{0,32},{1,33},{2,34},{3,35},{4,36},{5,37},{6,38},{7,39},{8,40},{9,... | collective-permute-start | bytes 442376 | tf_op jit(solution)/shard_map/ppermute | solution.py:46
  55.5 10.7 %collective-permute-start.15 = (bf16[2,2,24,768]{3,2,1,0:T(8,128)(2,1)S(1)}, bf16[2,2,24,768]{3,2,1,0:T(8,128)(2,1)S(1)}, u32[]{:S(2)}, u32[]{:S(2)}) collective-permute-start(bf16[2,2,24,768]{3,2,1,0:T(8,128)(2,1)S(1)} %get-tuple-element.13), channel_id=1, source_target_pairs={{0,16},{1,17},{2,18},{3,19},{4,20},{5,21},{6,22},{7,23},{8,24},{9,... | collective-permute-start | bytes 442376 | tf_op jit(solution)/shard_map/ppermute | solution.py:46
  66.2 65.4 %slice-start = ((s8[9437184]{0:T(1024)(128)(4,1)}), s8[4194304]{0:T(1024)(128)(4,1)S(1)}, s32[]{:S(2)}) async-start(s8[9437184]{0:T(1024)(128)(4,1)} %bitcast.168), calls=%async_computation.2 | async-start | bytes 8388608
  74.1 57.5 %slice-start.1 = ((s8[9437184]{0:T(1024)(128)(4,1)}), s8[4194304]{0:T(1024)(128)(4,1)S(1)}, s32[]{:S(2)}) async-start(s8[9437184]{0:T(1024)(128)(4,1)} %bitcast.168), calls=%async_computation.3 | async-start | bytes 8388608
  74.2 57.5 %slice-start.2 = ((s8[9437184]{0:T(1024)(128)(4,1)}), s8[1048576]{0:T(1024)(128)(4,1)S(1)}, s32[]{:S(2)}) async-start(s8[9437184]{0:T(1024)(128)(4,1)} %bitcast.168), calls=%async_computation.4 | async-start | bytes 2097152
  82.7 73.4 %collective-permute-start.6 = (bf16[192,6144]{1,0:T(8,128)(2,1)}, bf16[192,6144]{1,0:T(8,128)(2,1)S(1)}, u32[]{:S(2)}, u32[]{:S(2)}) collective-permute-start(bf16[192,6144]{1,0:T(8,128)(2,1)} %convolution_convert_fusion), channel_id=1, source_target_pairs={{0,1},{1,0},{2,3},{3,2},{4,5},{5,4},{6,7},{7,6},{8,9},{9,8},{10,11... | collective-permute-start | bytes 7077896 | tf_op jit(solution)/shard_map/ppermute | solution.py:46
  83.6 41.0 %collective-permute-start.16 = (bf16[2,192,768]{2,1,0:T(8,128)(2,1)S(1)}, bf16[2,192,768]{2,1,0:T(8,128)(2,1)S(1)}, u32[]{:S(2)}, u32[]{:S(2)}) collective-permute-start(bf16[2,192,768]{2,1,0:T(8,128)(2,1)S(1)} %bitcast.149), channel_id=1, source_target_pairs={{0,2},{1,3},{2,0},{3,1},{4,6},{5,7},{6,4},{7,5},{8,10},{9,11},{10,... | collective-permute-start | bytes 1769480 | tf_op jit(solution)/shard_map/ppermute | solution.py:46
  125.6 52.4 %collective-permute-start.19 = (bf16[2,192,768]{2,1,0:T(8,128)(2,1)}, bf16[2,192,768]{2,1,0:T(8,128)(2,1)}, u32[]{:S(2)}, u32[]{:S(2)}) collective-permute-start(bf16[2,192,768]{2,1,0:T(8,128)(2,1)} %get-tuple-element.10), channel_id=1, source_target_pairs={{0,4},{1,5},{2,6},{3,7},{4,8},{5,9},{6,10},{7,11},{8,12},{9,13},{1... | collective-permute-start | bytes 1769480 | tf_op jit(solution)/shard_map/ppermute | solution.py:46
  126.4 52.7 %collective-permute-start.17 = (bf16[2,192,768]{2,1,0:T(8,128)(2,1)}, bf16[2,192,768]{2,1,0:T(8,128)(2,1)}, u32[]{:S(2)}, u32[]{:S(2)}) collective-permute-start(bf16[2,192,768]{2,1,0:T(8,128)(2,1)} %get-tuple-element.10), channel_id=1, source_target_pairs={{0,12},{1,13},{2,14},{3,15},{4,0},{5,1},{6,2},{7,3},{8,4},{9,5},{1... | collective-permute-start | bytes 1769480 | tf_op jit(solution)/shard_map/ppermute | solution.py:46
  129.0 26.2 %collective-permute-start.24 = (bf16[2,192,768]{2,1,0:T(8,128)(2,1)S(1)}, bf16[2,192,768]{2,1,0:T(8,128)(2,1)S(1)}, u32[]{:S(2)}, u32[]{:S(2)}) collective-permute-start(bf16[2,192,768]{2,1,0:T(8,128)(2,1)S(1)} %get-tuple-element.11), channel_id=1, source_target_pairs={{0,4},{1,5},{2,6},{3,7},{4,8},{5,9},{6,10},{7,11},{8,12},{9,13},{1... | collective-permute-start | bytes 1769480 | tf_op jit(solution)/shard_map/ppermute | solution.py:46
  129.0 35.0 %collective-permute-start.22 = (bf16[2,192,768]{2,1,0:T(8,128)(2,1)S(1)}, bf16[2,192,768]{2,1,0:T(8,128)(2,1)S(1)}, u32[]{:S(2)}, u32[]{:S(2)}) collective-permute-start(bf16[2,192,768]{2,1,0:T(8,128)(2,1)S(1)} %get-tuple-element.11), channel_id=1, source_target_pairs={{0,12},{1,13},{2,14},{3,15},{4,0},{5,1},{6,2},{7,3},{8,4},{9,5},{1... | collective-permute-start | bytes 1769480 | tf_op jit(solution)/shard_map/ppermute | solution.py:46
  155.1 0.9 copy-start.2
  155.9 24.7 %collective-permute-start.25 = (bf16[192,768]{1,0:T(8,128)(2,1)}, bf16[192,768]{1,0:T(8,128)(2,1)}, u32[]{:S(2)}, u32[]{:S(2)}) collective-permute-start(bf16[192,768]{1,0:T(8,128)(2,1)} %slice_bitcast_fusion.1), channel_id=1, source_target_pairs={{0,4},{1,5},{2,6},{3,7},{4,8},{5,9},{6,10},{7,11},{8,12},{9,13},{1... | collective-permute-start | bytes 884744 | tf_op jit(solution)/shard_map/ppermute | solution.py:46
  164.0 9.1 %collective-permute-start.7 = (bf16[24,6144]{1,0:T(8,128)(2,1)}, bf16[24,6144]{1,0:T(8,128)(2,1)}, u32[]{:S(2)}, u32[]{:S(2)}) collective-permute-start(bf16[24,6144]{1,0:T(8,128)(2,1)} %get-tuple-element.5), channel_id=1, source_target_pairs={{0,4},{1,5},{2,6},{3,7},{4,8},{5,9},{6,10},{7,11},{8,12},{9,13},{1... | collective-permute-start | bytes 884744 | tf_op jit(solution)/shard_map/ppermute | solution.py:46
  164.0 2.7 %copy-start.4 = (bf16[2,192,768]{2,1,0:T(8,128)(2,1)}, bf16[2,192,768]{2,1,0:T(8,128)(2,1)S(1)}, u32[]{:S(2)}) copy-start(bf16[2,192,768]{2,1,0:T(8,128)(2,1)S(1)} %collective-permute-done.22) | copy-start | bytes 1769476
  164.0 10.1 %collective-permute-start.9 = (bf16[24,6144]{1,0:T(8,128)(2,1)}, bf16[24,6144]{1,0:T(8,128)(2,1)}, u32[]{:S(2)}, u32[]{:S(2)}) collective-permute-start(bf16[24,6144]{1,0:T(8,128)(2,1)} %get-tuple-element.6), channel_id=1, source_target_pairs={{0,12},{1,13},{2,14},{3,15},{4,0},{5,1},{6,2},{7,3},{8,4},{9,5},{1... | collective-permute-start | bytes 884744 | tf_op jit(solution)/shard_map/ppermute | solution.py:46
  168.3 9.6 %copy-start.6 = (bf16[1,24,6144]{2,1,0:T(8,128)(2,1)S(1)}, bf16[1,24,6144]{2,1,0:T(8,128)(2,1)}, u32[]{:S(2)}) copy-start(bf16[1,24,6144]{2,1,0:T(8,128)(2,1)} %get-tuple-element.8) | copy-start | bytes 884740
  173.1 9.9 %collective-permute-start.23 = (bf16[192,768]{1,0:T(8,128)(2,1)}, bf16[192,768]{1,0:T(8,128)(2,1)S(1)}, u32[]{:S(2)}, u32[]{:S(2)}) collective-permute-start(bf16[192,768]{1,0:T(8,128)(2,1)} %slice_bitcast_fusion.2), channel_id=1, source_target_pairs={{0,12},{1,13},{2,14},{3,15},{4,0},{5,1},{6,2},{7,3},{8,4},{9,5},{1... | collective-permute-start | bytes 884744 | tf_op jit(solution)/shard_map/ppermute | solution.py:46
  175.3 8.6 %copy-start.3 = (bf16[2,192,768]{2,1,0:T(8,128)(2,1)S(1)}, bf16[2,192,768]{2,1,0:T(8,128)(2,1)}, u32[]{:S(2)}) copy-start(bf16[2,192,768]{2,1,0:T(8,128)(2,1)} %copy-done.2) | copy-start | bytes 1769476
  175.3 8.6 %copy-start.5 = (bf16[2,192,768]{2,1,0:T(8,128)(2,1)S(1)}, bf16[2,192,768]{2,1,0:T(8,128)(2,1)}, u32[]{:S(2)}) copy-start(bf16[2,192,768]{2,1,0:T(8,128)(2,1)} %copy-done.4) | copy-start | bytes 1769476
  176.5 16.2 %collective-permute-start.10 = (bf16[2,24,6144]{2,1,0:T(8,128)(2,1)S(1)}, bf16[2,24,6144]{2,1,0:T(8,128)(2,1)S(1)}, u32[]{:S(2)}, u32[]{:S(2)}) collective-permute-start(bf16[2,24,6144]{2,1,0:T(8,128)(2,1)S(1)} %pad_maximum_fusion.6), channel_id=1, source_target_pairs={{0,12},{1,13},{2,14},{3,15},{4,0},{5,1},{6,2},{7,3},{8,4},{9,5},{1... | collective-permute-start | bytes 1769480 | tf_op jit(solution)/shard_map/ppermute | solution.py:46
  177.9 14.7 %collective-permute-start.8 = (bf16[2,24,6144]{2,1,0:T(8,128)(2,1)S(1)}, bf16[2,24,6144]{2,1,0:T(8,128)(2,1)S(1)}, u32[]{:S(2)}, u32[]{:S(2)}) collective-permute-start(bf16[2,24,6144]{2,1,0:T(8,128)(2,1)S(1)} %pad_maximum_fusion.5), channel_id=1, source_target_pairs={{0,4},{1,5},{2,6},{3,7},{4,8},{5,9},{6,10},{7,11},{8,12},{9,13},{1... | collective-permute-start | bytes 1769480 | tf_op jit(solution)/shard_map/ppermute | solution.py:46
  179.1 18.9 %collective-permute-start.20 = (bf16[192,768]{1,0:T(8,128)(2,1)S(1)}, bf16[192,768]{1,0:T(8,128)(2,1)S(1)}, u32[]{:S(2)}, u32[]{:S(2)}) collective-permute-start(bf16[192,768]{1,0:T(8,128)(2,1)S(1)} %slice_bitcast_fusion.3), channel_id=1, source_target_pairs={{0,4},{1,5},{2,6},{3,7},{4,8},{5,9},{6,10},{7,11},{8,12},{9,13},{1... | collective-permute-start | bytes 884744 | tf_op jit(solution)/shard_map/ppermute | solution.py:46
  180.6 18.4 %collective-permute-start.18 = (bf16[192,768]{1,0:T(8,128)(2,1)S(1)}, bf16[192,768]{1,0:T(8,128)(2,1)S(1)}, u32[]{:S(2)}, u32[]{:S(2)}) collective-permute-start(bf16[192,768]{1,0:T(8,128)(2,1)S(1)} %slice_bitcast_fusion.4), channel_id=1, source_target_pairs={{0,12},{1,13},{2,14},{3,15},{4,0},{5,1},{6,2},{7,3},{8,4},{9,5},{1... | collective-permute-start | bytes 884744 | tf_op jit(solution)/shard_map/ppermute | solution.py:46
  184.3 8.6 %copy-start = (bf16[4,2,192,768]{3,2,1,0:T(8,128)(2,1)}, bf16[4,2,192,768]{3,2,1,0:T(8,128)(2,1)S(1)}, u32[]{:S(2)}) copy-start(bf16[4,2,192,768]{3,2,1,0:T(8,128)(2,1)S(1)} %pad_maximum_fusion.2) | copy-start | bytes 7077892
  184.3 46.7 %collective-permute-start.26 = (bf16[1536,768]{1,0:T(8,128)(2,1)S(1)}, bf16[1536,768]{1,0:T(8,128)(2,1)}, u32[]{:S(2)}, u32[]{:S(2)}) collective-permute-start(bf16[1536,768]{1,0:T(8,128)(2,1)S(1)} %bitcast.153), channel_id=1, source_target_pairs={{0,1},{1,0},{2,3},{3,2},{4,5},{5,4},{6,7},{7,6},{8,9},{9,8},{10,11... | collective-permute-start | bytes 7077896 | tf_op jit(solution)/shard_map/ppermute | solution.py:46
  192.9 37.3 %collective-permute-start.11 = (bf16[24,6144]{1,0:T(8,128)(2,1)S(1)}, bf16[24,6144]{1,0:T(8,128)(2,1)S(1)}, u32[]{:S(2)}, u32[]{:S(2)}) collective-permute-start(bf16[24,6144]{1,0:T(8,128)(2,1)S(1)} %fusion.39), channel_id=1, source_target_pairs={{0,2},{1,3},{2,0},{3,1},{4,6},{5,7},{6,4},{7,5},{8,10},{9,11},{10,... | collective-permute-start | bytes 884744 | tf_op jit(solution)/shard_map/ppermute | solution.py:46
  199.1 32.0 %copy-start.1 = (bf16[4,2,192,768]{3,2,1,0:T(8,128)(2,1)S(1)}, bf16[4,2,192,768]{3,2,1,0:T(8,128)(2,1)}, u32[]{:S(2)}) copy-start(bf16[4,2,192,768]{3,2,1,0:T(8,128)(2,1)} %copy-done) | copy-start | bytes 7077892
  202.2 37.2 %collective-permute-start.21 = (bf16[1536,768]{1,0:T(8,128)(2,1)}, bf16[1536,768]{1,0:T(8,128)(2,1)}, u32[]{:S(2)}, u32[]{:S(2)}) collective-permute-start(bf16[1536,768]{1,0:T(8,128)(2,1)} %bitcast.50), channel_id=1, source_target_pairs={{0,1},{1,0},{2,3},{3,2},{4,5},{5,4},{6,7},{7,6},{8,9},{9,8},{10,11... | collective-permute-start | bytes 7077896 | tf_op jit(solution)/shard_map/ppermute | solution.py:46
Sparse Core Ops, SparseCore 0:
  51.4 58.9 all-gather.4
  168.4 54.3 all-gather.2
